TPU v7x, 32 devices: a whole 2x2x4 slice. The times are simulated.
32 devices in a mesh: groups: 2 (over y), tensor: 4 (over z), fsdp: 2 (over x), dp: 2 (over core).
Axes of the slice: x: 2, y: 2, z: 4, core: 2. Of those that a mesh axis runs over, the one named last changes fastest.
Arguments:
- tokens: bfloat16 [8, 256, 8192], P(('groups', 'fsdp', 'dp')), parts along dimension 0, may hold values from -6 to 6
- teacher: bfloat16 [8, 256, 8192], P(('groups', 'fsdp', 'dp')), parts along dimension 0, may hold values from -3 to 3
- in_blocks: bfloat16 [8192, 4608], P('fsdp', 'tensor'), may hold values from -0.09375 to 0.09375
- in_columns: int32 [64, 36], P('fsdp', 'tensor'), may hold values from 0 to 17, as said below
- step_weight: bfloat16 [8192, 128], P('fsdp', 'tensor'), may hold values from -0.0625 to 0.0625
- out_blocks: bfloat16 [8192, 4096], P('fsdp', 'tensor'), may hold values from -0.09375 to 0.09375
- out_columns: int32 [64, 32], P('fsdp', 'tensor'), may hold values from 0 to 15, as said below
- conv_weight: float32 [4, 9216], P(None, 'tensor'), may hold values from -3 to 3
- step_bias: float32 [128], P('tensor'), may hold values from -2 to 0.5
- decay_rate: float32 [128], P('tensor'), may hold values from 0.005 to 0.3
- skip_gain: float32 [128], P('tensor'), may hold values from 0.5 to 1.5
- norm_gain: float32 [8192], P('tensor'), may hold values from 0.5 to 1.5
Outputs:
- sq_error: float32 [8, 256], P(('groups', 'fsdp', 'dp')), parts along dimension 0
- in_grad: float32 [16384, 4608], P(('groups', 'fsdp', 'dp'), 'tensor'), parts along dimension 0
- out_grad: float32 [16384, 4096], P(('groups', 'fsdp', 'dp'), 'tensor'), parts along dimension 0
There are 2 independent parts, one for each index of `groups`. A program takes and returns all parts, laid end to end along the dimension named above; an argument that names none is the same for every part. Nothing has to cross between parts.
Inputs may be any that keep to these rules, and one draw needn't show every extreme that they name: `in_columns`: in every row the 9 entries g * 9 to g * 9 + 8 are distinct, for every group g. `out_columns`: in every row the 8 entries g * 8 to g * 8 + 7 are distinct, for every group g.
All inputs are finite; a program needn't handle non-finite values.
Results may differ from a plain program's by a relative error of at most 0.014.
Values may be sent and summed in bfloat16 or wider, within the bound.
A program may use at most 320 MiB of HBM per device.

v0:
```python
import math

import jax
import jax.numpy as jnp
from jax import lax
from jax.sharding import PartitionSpec as P

BLOCK = 128


def spread_blocks(blocks, chosen, group_width):
    block_rows = chosen.shape[0]
    keep_count = chosen.shape[1]
    picked = (chosen[:, :, None] == jnp.arange(group_width, dtype=jnp.int32)[None, None, :]).astype(
        jnp.bfloat16
    )
    tile_grid = blocks.reshape(block_rows, BLOCK, keep_count, BLOCK)
    dense_grid = jnp.einsum("rkc,rikj->ricj", picked, tile_grid, preferred_element_type=jnp.float32)
    return dense_grid.astype(jnp.bfloat16).reshape(block_rows * BLOCK, group_width * BLOCK)


def keep_blocks(dense_grad, chosen):
    block_rows = chosen.shape[0]
    keep_count = chosen.shape[1]
    group_width = dense_grad.shape[1] // BLOCK
    tile_grid = dense_grad.reshape(block_rows, BLOCK, group_width, BLOCK)
    selected = jnp.take_along_axis(tile_grid, chosen[:, None, :, None], axis=2)
    return selected.reshape(block_rows * BLOCK, keep_count * BLOCK)


def state_mixer(projected, step_raw, conv_taps, step_bias, decay_rate, skip_gain, norm_gain):
    seq_steps = projected.shape[0]
    chan_count = projected.shape[1]
    inner_width = norm_gain.shape[0]
    head_count = step_bias.shape[0]
    head_width = inner_width // head_count
    state_size = (chan_count - inner_width) // 2
    taps = conv_taps.shape[0]
    padded = jnp.concatenate([jnp.zeros((taps - 1, chan_count), jnp.float32), projected], 0)
    conv_sum = jnp.zeros((seq_steps, chan_count), jnp.float32)
    for offset in range(taps):
        conv_sum = conv_sum + conv_taps[offset][None, :] * padded[offset : offset + seq_steps]
    activated = jax.nn.silu(conv_sum)
    head_inputs = activated[:, :inner_width].reshape(seq_steps, head_count, head_width)
    state_in = activated[:, inner_width : inner_width + state_size]
    state_out = activated[:, inner_width + state_size :]
    step_size = jax.nn.softplus(step_raw + step_bias[None, :])
    log_decay = jnp.cumsum(-decay_rate[None, :] * step_size, axis=0)
    scores = jnp.dot(state_out, state_in.T, precision=lax.Precision.HIGHEST)
    later = (jnp.arange(seq_steps)[:, None] >= jnp.arange(seq_steps)[None, :])[:, :, None]
    log_gap = log_decay[:, None, :] - log_decay[None, :, :]
    decay = jnp.where(later, jnp.exp(jnp.where(later, log_gap, 0.0)), 0.0)
    weights = scores[:, :, None] * decay * step_size[None, :, :]
    mixed = jnp.einsum("tsh,shp->thp", weights, head_inputs, precision=lax.Precision.HIGHEST)
    mixed = mixed + skip_gain[None, :, None] * head_inputs
    flat = mixed.reshape(seq_steps, inner_width)
    scale = lax.rsqrt(jnp.mean(flat * flat, axis=1, keepdims=True) + 1e-05)
    return flat * scale * norm_gain[None, :]


def local(
    tokens,
    teacher,
    in_blocks,
    in_columns,
    step_weight,
    out_blocks,
    out_columns,
    conv_weight,
    step_bias,
    decay_rate,
    skip_gain,
    norm_gain,
):
    full_seq = tokens[0]
    seq_len = full_seq.shape[0]
    model_width = full_seq.shape[1]
    local_rows = in_columns.shape[0]
    keep_in = in_columns.shape[1]
    keep_out = out_columns.shape[1]
    head_count = step_bias.shape[0]
    packed = (
        in_blocks.reshape(local_rows, -1),
        out_blocks.reshape(local_rows, -1),
        step_weight.reshape(local_rows, -1),
        jnp.concatenate([in_columns, out_columns], 1).astype(jnp.bfloat16),
    )
    in_all, out_all, step_all, picks = (
        lax.all_gather(packed[0], "fsdp", axis=0, tiled=True),
        lax.all_gather(packed[1], "fsdp", axis=0, tiled=True),
        lax.all_gather(packed[2], "fsdp", axis=0, tiled=True),
        lax.all_gather(packed[3], "fsdp", axis=0, tiled=True),
    )
    picks = picks.astype(jnp.int32)
    in_pick = picks[:, :keep_in]
    out_pick = picks[:, keep_in:]
    w_in = spread_blocks(in_all.reshape(-1, keep_in * BLOCK), in_pick, 2 * keep_in)
    w_out = spread_blocks(out_all.reshape(-1, keep_out * BLOCK), out_pick, 2 * keep_out)
    projected_sum = jnp.dot(full_seq, w_in, preferred_element_type=jnp.float32)
    step_raw = jnp.dot(
        full_seq, step_all.reshape(model_width, head_count), preferred_element_type=jnp.float32
    )
    projected = projected_sum.astype(jnp.bfloat16)

    def local_mix(values):
        return state_mixer(
            values, step_raw, conv_weight, step_bias, decay_rate, skip_gain, norm_gain
        )

    normed_exact, pull_back = jax.vjp(local_mix, projected.astype(jnp.float32))
    normed = normed_exact.astype(jnp.bfloat16)
    group_terms = lax.dot_general(
        normed, w_out, (((1,), (1,)), ((), ())), preferred_element_type=jnp.float32
    )
    student = lax.psum(group_terms.astype(jnp.bfloat16), "tensor")
    gap = student.astype(jnp.float32) - teacher[0].astype(jnp.float32)
    sq_error = jnp.mean(gap * gap, axis=1)[None, :]
    total_tokens = seq_len * lax.axis_size("fsdp") * lax.axis_size("dp")
    grad_seq = (gap * (1.0 / math.sqrt(total_tokens))).astype(jnp.bfloat16)
    d_normed = jnp.dot(grad_seq, w_out, preferred_element_type=jnp.float32)
    d_projected = pull_back(d_normed)[0].astype(jnp.bfloat16)
    out_dense = lax.dot_general(
        grad_seq, normed, (((0,), (0,)), ((), ())), preferred_element_type=jnp.float32
    )
    out_term = keep_blocks(out_dense, out_pick)
    in_dense = lax.dot_general(
        full_seq, d_projected, (((0,), (0,)), ((), ())), preferred_element_type=jnp.float32
    )
    in_term = keep_blocks(in_dense, in_pick)
    in_grad, out_grad = (
        lax.psum_scatter(
            in_term.astype(jnp.bfloat16), ("fsdp", "dp"), scatter_dimension=0, tiled=True
        ).astype(jnp.float32),
        lax.psum_scatter(
            out_term.astype(jnp.bfloat16), ("fsdp", "dp"), scatter_dimension=0, tiled=True
        ).astype(jnp.float32),
    )
    return (sq_error, in_grad, out_grad)


def solution(mesh):
    placed = (
        P(("groups", "fsdp", "dp"), None, None),
        P(("groups", "fsdp", "dp"), None, None),
        P("fsdp", "tensor"),
        P("fsdp", "tensor"),
        P("fsdp", "tensor"),
        P("fsdp", "tensor"),
        P("fsdp", "tensor"),
        P(None, "tensor"),
        P("tensor"),
        P("tensor"),
        P("tensor"),
        P("tensor"),
    )
    return jax.shard_map(
        local,
        mesh=mesh,
        in_specs=placed,
        out_specs=(
            P(("groups", "fsdp", "dp"), None),
            P(("groups", "fsdp", "dp"), "tensor"),
            P(("groups", "fsdp", "dp"), "tensor"),
        ),
        check_vma=False,
    )
```

profile of v0, /device:TPU:0, one launch (start us, length us, event | category | flops | bytes accessed | tf_op | source)
XLA Modules:
  0.0 1211.1 jit_solution(17175752381810831582)
XLA Ops:
  7.2 8.9 reshape.175
  16.2 9.7 reshape.168
  34.0 14.4 %all_gather.14 = bf16[64,4096]{1,0:T(8,128)(2,1)S(1)} all-gather(bf16[32,4096]{1,0:T(8,128)(2,1)S(1)} %reshape.171), channel_id=1, replica_groups=mesh['groups'=2,'tensor'=4,'fsdp'=2,'dp'=2] {'fsdp'}, dimensions={0}, use_global_device_ids=true | all-gather | bytes 786432 | tf_op jit(solution)/shard_map/all_gather | solution.py:91
  54.9 167.1 %all-gather.6.cloned.1.call-done = bf16[64,131072]{1,0:T(8,128)(2,1)} async-done(((bf16[32,131072]{1,0:T(8,128)(2,1)}), bf16[64,131072]{1,0:T(8,128)(2,1)}) %all-gather.6.cloned.1.call-update) | async-done | bytes 16777232 | tf_op jit(solution)/shard_map/all_gather | solution.py:90
  222.0 16.2 %copy.83 = bf16[8,8,1024,128]{3,2,1,0:T(8,128)(2,1)} copy(bf16[8,8,1024,128]{3,1,2,0:T(8,128)(2,1)} %bitcast.190) | data formatting | bytes 33554432
  238.3 21.4 %convolution_convert_fusion.1 = bf16[64,16,128,128]{3,1,2,0:T(8,128)(2,1)} fusion(bf16[64,128,8,128]{3,2,1,0:T(8,128)(2,1)} %bitcast.180, s32[64,8]{1,0:T(8,128)S(1)} %copy.58), kind=kOutput, calls=%fused_computation.15 | convolution fusion | flops 285220864 | bytes 50333696 | tf_op jit(solution)/shard_map/rkc,rikj->ricj/dot_general | solution.py:18
  259.6 190.3 %all-gather.4.cloned.1.call-done = bf16[64,147456]{1,0:T(8,128)(2,1)} async-done(((bf16[32,147456]{1,0:T(8,128)(2,1)}), bf16[64,147456]{1,0:T(8,128)(2,1)}) %all-gather.4.cloned.1.call-update) | async-done | bytes 18874384 | tf_op jit(solution)/shard_map/all_gather | solution.py:89
  450.0 21.3 %reshape_reshape.6 = bf16[64,128,9,128]{3,2,1,0:T(8,128)(2,1)} reshape(bf16[64,147456]{1,0:T(8,128)(2,1)} %all-gather.4.cloned.1.call-done) | data formatting | bytes 37748736 | tf_op jit(solution)/shard_map/reshape;reshape | solution.py:17
  471.3 31.5 %convolution_convert_fusion = bf16[64,18,128,128]{3,1,2,0:T(8,128)(2,1)} fusion(bf16[64,128,9,128]{3,2,1,0:T(8,128)(2,1)} %reshape_reshape.6, s32[64,9]{1,0:T(8,128)S(1)} %copy.52), kind=kOutput, calls=%fused_computation.13 | convolution fusion | flops 358623360 | bytes 56625408 | tf_op jit(solution)/shard_map/rkc,rikj->ricj/dot_general | solution.py:18
  502.8 22.6 %fusion.44 = f32[256,2304]{1,0:T(8,128)} fusion(bf16[1024,8,18,128]{3,2,1,0:T(8,128)(2,1)} %bitcast.188, bf16[1,256,8192]{2,1,0:T(8,128)(2,1)} %param.12), kind=kOutput, calls=%fused_computation.49 | convolution fusion | flops 9664856064 | bytes 44302336 | tf_op jit(solution)/shard_map/dot_general | solution.py:99
  525.4 6.9 fusion.55
  537.2 12.2 %multiply_reduce_fusion.2 = (f32[256]{0:T(256)S(1)}, f32[256,32,64]{0,2,1:T(8,128)S(1)}) fusion(f32[256,32,64]{0,2,1:T(8,128)} %bitcast.193, f32[32]{0:T(128)S(1)} %copy-done.23, f32[256,32]{0,1:T(8,128)S(1)} %get-tuple-element.24, f32[256,32]{0,1:T(8,128)S(1)} %bitcast_bitcast_fusion, f32[256,256]{1,0:T(8,128)S(1)} %fusion.71, ...), kind=kOutput, calls=%fused_computation.69 | convolution fusion | flops 1623195392 | bytes 4588672 | tf_op jit(solution)/shard_map/jvp(tsh,shp->thp)/dot_general | solution.py:54
  551.1 22.6 %fusion.11 = bf16[256,8192]{1,0:T(8,128)(2,1)} fusion(bf16[256,2048]{0,1:T(8,128)(2,1)S(1)} %bitcast.199, bf16[1024,8,16,128]{3,2,1,0:T(8,128)(2,1)} %bitcast.186), kind=kOutput, calls=%fused_computation.20 | convolution fusion | flops 8592031744 | bytes 38797312 | tf_op jit(solution)/shard_map/dot_general | solution.py:112
  577.3 151.7 %all-reduce.10.cloned.1.call-done = bf16[256,8192]{1,0:T(8,128)(2,1)} async-done(((bf16[256,8192]{1,0:T(8,128)(2,1)}), bf16[256,8192]{1,0:T(8,128)(2,1)}) %all-reduce.10.cloned.1.call-update) | async-done | bytes 4194320 | tf_op jit(solution)/shard_map/psum | solution.py:115
  729.0 24.0 %multiply_reduce_fusion.1 = (f32[256]{0:T(256)S(1)}, f32[256,2048]{1,0:T(8,128)S(1)}) fusion(f32[256,2048]{1,0:T(8,128)} %copy.61, f32[2048]{0:T(1024)S(1)} %copy-done.11, bf16[1024,8,16,128]{3,2,1,0:T(8,128)(2,1)} %bitcast.187, bf16[256,8192]{1,0:T(8,128)(2,1)} %all-reduce.10.cloned.1.call-done, bf16[1,256,8192]{2,1,0:T(8,128)(2,1)} %param.13), kind=kOutput, calls=%fused_computation.67 | convolution fusion | flops 8601993216 | bytes 46146560 | tf_op jit(solution)/shard_map/dot_general | solution.py:120
  769.5 15.8 %fusion.88 = bf16[64,128,16,128]{3,1,2,0:T(8,128)(2,1)} fusion(bf16[64,128,256,1]{2,1,3,0:T(8,128)(2,1)} %bitcast.189, bf16[16,128,256,1]{2,1,0,3:T(8,128)(2,1)S(1)} %bitcast.192), kind=kOutput, calls=%fused_computation.124 | convolution fusion | flops 8589934592 | bytes 38797312 | tf_op jit(solution)/shard_map/dot_general | solution.py:122
  785.3 18.2 %gather_fusion.1 = bf16[512,128,128]{2,1,0:T(8,128)(2,1)} fusion(bf16[64,128,16,128]{3,1,2,0:T(8,128)(2,1)} %fusion.88, s32[512]{0:T(512)S(1)} %reshape.190), kind=kCustom, calls=%fused_computation.1 | custom fusion | bytes 33558528 | tf_op jit(solution)/shard_map/jit(take_along_axis)/gather | solution.py:27
  803.5 9.4 fusion.10
  812.9 11.5 copy.72
  824.5 9.3 copy.117
  837.1 10.6 bitcast_add_fusion
  851.2 12.4 %fusion.15 = f32[256,256]{1,0:T(8,128)S(1)} fusion(f32[256,32]{0,1:T(8,128)S(1)} %copy-done.9, f32[256,32]{0,1:T(8,128)S(1)} %copy-done.13, pred[256,256]{1,0:T(8,128)(4,1)S(1)} %iota_compare_fusion.2, f32[32,64,256]{2,1,0:T(8,128)} %bitcast.197, f32[256,32,64]{0,2,1:T(8,128)} %bitcast.194), kind=kOutput, calls=%fused_computation.24 | convolution fusion | flops 1623130112 | bytes 4587520 | tf_op jit(solution)/shard_map/transpose(jvp(tsh,shp->thp))/dot_general | solution.py:54
  868.7 20.5 %convolution_bitcast_fusion = bf16[288,8,64,128]{3,1,2,0:T(8,128)(2,1)} fusion(bf16[1,256,8192]{2,1,0:T(8,128)(2,1)} %param.12, f32[256,2304]{1,0:T(8,128)} %get-tuple-element.21, f32[256,2304]{1,0:T(8,128)} %get-tuple-element.20, f32[256,2304]{1,0:T(8,128)} %get-tuple-element.19, f32[256,2304]{1,0:T(8,128)S(1)} %get-tuple-element.13), kind=kOutput, calls=%fused_computation.14 | convolution fusion | flops 9666035712 | bytes 51380224 | tf_op jit(solution)/shard_map/dot_general | solution.py:126
  889.2 26.2 %copy.85 = bf16[288,8,64,128]{3,2,1,0:T(8,128)(2,1)} copy(bf16[288,8,64,128]{3,1,2,0:T(8,128)(2,1)} %convolution_bitcast_fusion) | data formatting | bytes 75497472
  915.4 48.2 %copy.65 = bf16[64,128,18,128]{3,1,2,0:T(8,128)(2,1)} copy(bf16[64,128,18,128]{1,0,3,2:T(8,128)(2,1)} %bitcast.178) | data formatting | bytes 75497472 | tf_op jit(solution)/shard_map/reshape | solution.py:26
  963.6 27.3 %gather_fusion = bf16[576,128,128]{2,1,0:T(8,128)(2,1)} fusion(bf16[64,128,18,128]{3,1,2,0:T(8,128)(2,1)} %copy.65, s32[576]{0:T(1024)S(1)} %reshape.184), kind=kCustom, calls=%fused_computation | custom fusion | bytes 37753344 | tf_op jit(solution)/shard_map/jit(take_along_axis)/gather | solution.py:27
  990.9 17.9 %fusion.9 = bf16[64,128,9,128]{3,1,2,0:T(8,128)(2,1)} fusion(bf16[64,9,128,128]{3,2,1,0:T(8,128)(2,1)} %bitcast.179, pred[64,9]{1,0:T(8,128)(4,1)S(1)} %copy.59), kind=kLoop, calls=%fused_computation.16 | loop fusion | flops 9437184 | bytes 37749312 | tf_op jit(solution)/shard_map/convert_element_type | solution.py:132
  1008.8 24.0 %copy.66 = bf16[64,128,9,128]{1,0,3,2:T(8,128)(2,1)} copy(bf16[64,128,9,128]{3,1,2,0:T(8,128)(2,1)} %fusion.9) | data formatting | bytes 37748736 | tf_op jit(solution)/shard_map/convert_element_type | solution.py:132
  1032.9 22.4 %copy.116 = bf16[144,8,64,128]{3,1,2,0:T(8,128)(2,1)} copy(bf16[144,8,64,128]{3,2,1,0:T(8,128)(2,1)} %bitcast.182) | data formatting | bytes 37748736
  1056.5 6.8 convert_element_type.91
  1063.3 133.4 %reduce-scatter.3.cloned.1.call-done = bf16[2048,1152]{0,1:T(8,128)(2,1)} async-done(((bf16[8192,1152]{0,1:T(8,128)(2,1)}), bf16[2048,1152]{0,1:T(8,128)(2,1)}) %reduce-scatter.3.cloned.1.call-update) | async-done | bytes 4718608 | tf_op jit(solution)/shard_map/reduce_scatter | solution.py:131
  1196.7 7.4 copy.73
  (114 shorter events, 54.3 us)
Async XLA Ops:
  7.2 214.9 %all-gather.6.cloned.1.call-start = ((), (), s32[]{:S(2)}) async-start(), calls=%async_computation.3 | async-start | bytes 25165824 | tf_op jit(solution)/shard_map/all_gather | solution.py:90
  16.1 433.9 %all-gather.4.cloned.1.call-start = ((), (), s32[]{:S(2)}) async-start(), calls=%async_computation.2 | async-start | bytes 28311552 | tf_op jit(solution)/shard_map/all_gather | solution.py:89
  25.8 0.7 copy-start.16
  25.8 0.7 copy-start.20
  25.8 6.6 copy-start.4
  25.9 703.1 %all-reduce.10.cloned.1.call-start = ((), (), s32[]{:S(2)}) async-start(), calls=%async_computation.4 | async-start | bytes 8388608 | tf_op jit(solution)/shard_map/psum | solution.py:115
  32.9 17.2 %copy-start.22 = (f32[32]{0:T(128)S(1)}, f32[32]{0:T(128)}, u32[]{:S(2)}) copy-start(f32[32]{0:T(128)} %param.21) | copy-start | bytes 388
  32.9 17.2 %copy-start.21 = (f32[32]{0:T(128)S(1)}, f32[32]{0:T(128)}, u32[]{:S(2)}) copy-start(f32[32]{0:T(128)} %param.20) | copy-start | bytes 388
  50.1 4.4 copy-start.10
  50.1 4.6 copy-start.7
  53.7 483.5 %copy-start.8 = (f32[256,32]{0,1:T(8,128)}, f32[256,32]{0,1:T(8,128)S(1)}, u32[]{:S(2)}) copy-start(f32[256,32]{0,1:T(8,128)S(1)} %get-tuple-element.24) | copy-start | bytes 98308
  54.9 482.3 %copy-start.12 = (f32[256,32]{0,1:T(8,128)}, f32[256,32]{0,1:T(8,128)S(1)}, u32[]{:S(2)}) copy-start(f32[256,32]{0,1:T(8,128)S(1)} %bitcast_bitcast_fusion) | copy-start | bytes 98308
  533.8 3.4 copy-start.23
  534.2 15.2 %copy-start.5 = (f32[256,256]{1,0:T(8,128)}, f32[256,256]{1,0:T(8,128)S(1)}, u32[]{:S(2)}) copy-start(f32[256,256]{1,0:T(8,128)S(1)} %fusion.71) | copy-start | bytes 786436
  549.4 0.6 copy-start.18
  549.5 1.3 copy-start.3
  550.0 1.1 copy-start.14
  573.8 155.2 %copy-start.11 = (f32[2048]{0:T(1024)S(1)}, f32[2048]{0:T(1024)}, u32[]{:S(2)}) copy-start(f32[2048]{0:T(1024)} %param.23) | copy-start | bytes 24580
  573.8 482.7 %reduce-scatter.5.cloned.1.call-start = ((), (), s32[]{:S(2)}) async-start(), calls=%async_computation.6 | async-start | bytes 20971520 | tf_op jit(solution)/shard_map/reduce_scatter | solution.py:134
  577.3 175.7 %copy-start.19 = (f32[256]{0:T(256)S(1)}, f32[256]{0:T(256)}, u32[]{:S(2)}) copy-start(f32[256]{0:T(256)} %copy-done.18) | copy-start | bytes 3076
  577.3 175.7 %copy-start.15 = (f32[256]{0:T(256)S(1)}, f32[256]{0:T(256)}, u32[]{:S(2)}) copy-start(f32[256]{0:T(256)} %copy-done.14) | copy-start | bytes 3076
  729.0 24.0 %copy-start.1 = (f32[256,2048]{1,0:T(8,128)S(1)}, f32[256,2048]{1,0:T(8,128)}, u32[]{:S(2)}) copy-start(f32[256,2048]{1,0:T(8,128)} %copy.61) | copy-start | bytes 6291460
  833.8 3.4 copy-start.6
  833.8 3.3 copy-start.9
  833.8 3.3 copy-start.13
  833.8 3.3 copy-start.24
  833.8 362.9 %reduce-scatter.3.cloned.1.call-start = ((), (), s32[]{:S(2)}) async-start(), calls=%async_computation.5 | async-start | bytes 23592960 | tf_op jit(solution)/shard_map/reduce_scatter | solution.py:131
  851.2 13.4 %copy-start = (f32[256,2304]{1,0:T(8,128)S(1)}, f32[256,2304]{1,0:T(8,128)}, u32[]{:S(2)}) copy-start(f32[256,2304]{1,0:T(8,128)} %get-tuple-element.16) | copy-start | bytes 7077892
  851.2 13.4 %copy-start.2 = (f32[256,2048]{1,0:T(8,128)S(1)}, f32[256,2048]{1,0:T(8,128)}, u32[]{:S(2)}) copy-start(f32[256,2048]{1,0:T(8,128)} %copy.63) | copy-start | bytes 6291460
  1055.3 0.7 copy-start.17
Sparse Core Ops, SparseCore 0:
  16.2 205.7 all-gather.5
  224.2 225.7 all-gather.3
  573.9 154.9 all-reduce.9
  833.9 125.1 reduce-scatter.4
  1055.4 141.2 reduce-scatter.2
where the time goes:
time: 1220 us; the launch traced here: 1210 us
  waiting for transfers between devices  643 us (53%)
  local copies, waits for them, and re-layouts  279 us (23%)
  matrix products  199 us (16%)
  other arithmetic  55.5 us (5%)
  blocking collectives  20.1 us (2%)
  between operations  14.6 us (1%)
    all_gather x1, waiting for transfers between devices, local(): lax.all_gather(packed[0], 'fsdp', axis=0, tiled=True)  190 us
    all_gather x1, waiting for transfers between devices, local(): lax.all_gather(packed[1], 'fsdp', axis=0, tiled=True)  167 us
    psum x1, waiting for transfers between devices, local(): student = lax.psum(group_terms.astype(jnp.bfloat16), 'tensor')  152 us
    reduce_scatter x1, waiting for transfers between devices, local(): lax.psum_scatter(in_term.astype(jnp.bfloat16), ('fsdp', 'dp'), scatter_di...  133 us
    unnamed x56, local copies, waits for them, and re-layouts  84.6 us
    dot_general x2, matrix products, spread_blocks(): jnp.einsum('rkc,rikj->ricj', picked, tile_grid, preferred_element_type=jn...  52.9 us
    reshape x1, local copies, waits for them, and re-layouts, keep_blocks(): tile_grid = dense_grad.reshape(block_rows, BLOCK, group_width, BLOCK)  48.2 us
    gather x6, local copies, waits for them, and re-layouts, keep_blocks(): selected = jnp.take_along_axis(tile_grid, chosen[:, None, :, None], axis=2)  45.9 us
  transfers between devices with their start and end apart: 5, of which 4 were waited for; matrix products, arithmetic and copies ran while one was open for 24% of the time, Pallas kernels for 0%

commit v1 on v0

v1 whole, which is shorter than its diff:
```python
import functools
import math

import jax
import jax.numpy as jnp
from jax import lax
from jax.experimental import pallas as pl
from jax.experimental.pallas import tpu as pltpu
from jax.sharding import PartitionSpec as P

BLOCK = 128
VMEM = 48 * 1024 * 1024


def chunk_of(size, most):
    chunk = min(size, most)
    while size % chunk:
        chunk //= 2
    return chunk


def spread_into(dense_ref, blocks_ref, cols_ref, first, keep):
    dense_ref[...] = jnp.zeros_like(dense_ref)
    for i in range(dense_ref.shape[0] // BLOCK):
        rows = slice(i * BLOCK, (i + 1) * BLOCK)
        for k in range(keep):
            c = cols_ref[(first + i) * keep + k]
            dense_ref[rows, pl.ds(pl.multiple_of(c * BLOCK, BLOCK), BLOCK)] = blocks_ref[
                rows, k * BLOCK : (k + 1) * BLOCK
            ]


def contract_kernel(keep, cols_ref, x_ref, blocks_ref, out_ref, dense_ref, acc_ref):
    j = pl.program_id(0)
    spread_into(dense_ref, blocks_ref, cols_ref, j * (dense_ref.shape[0] // BLOCK), keep)
    term = jnp.dot(x_ref[...], dense_ref[...], preferred_element_type=jnp.float32)

    @pl.when(j == 0)
    def _():
        acc_ref[...] = term

    @pl.when(j > 0)
    def _():
        acc_ref[...] += term

    @pl.when(j == pl.num_programs(0) - 1)
    def _():
        out_ref[...] = acc_ref[...].astype(out_ref.dtype)


def contract(x, blocks, cols, out_dtype):
    seq, depth = x.shape
    keep = cols.shape[1]
    width = 2 * keep * BLOCK
    step = chunk_of(depth, 512)
    return pl.pallas_call(
        functools.partial(contract_kernel, keep),
        out_shape=jax.ShapeDtypeStruct((seq, width), out_dtype),
        grid_spec=pltpu.PrefetchScalarGridSpec(
            num_scalar_prefetch=1,
            grid=(depth // step,),
            in_specs=[
                pl.BlockSpec((seq, step), lambda j, c: (0, j)),
                pl.BlockSpec((step, keep * BLOCK), lambda j, c: (j, 0)),
            ],
            out_specs=pl.BlockSpec((seq, width), lambda j, c: (0, 0)),
            scratch_shapes=[
                pltpu.VMEM((step, width), jnp.bfloat16),
                pltpu.VMEM((seq, width), jnp.float32),
            ],
        ),
        compiler_params=pltpu.CompilerParams(vmem_limit_bytes=VMEM),
        cost_estimate=pl.CostEstimate(
            flops=2 * seq * depth * width,
            bytes_accessed=2 * depth * (seq + keep * BLOCK) + 4 * seq * width,
            transcendentals=0,
        ),
    )(cols.reshape(-1), x, blocks)


def expand_kernel(keep, cols_ref, x_ref, blocks_ref, out_ref, dense_ref):
    j = pl.program_id(0)
    spread_into(dense_ref, blocks_ref, cols_ref, j * (dense_ref.shape[0] // BLOCK), keep)
    out_ref[...] = lax.dot_general(
        x_ref[...], dense_ref[...], (((1,), (1,)), ((), ())), preferred_element_type=jnp.float32
    ).astype(out_ref.dtype)


def expand(x, blocks, cols):
    seq, width = x.shape
    rows = blocks.shape[0]
    keep = cols.shape[1]
    step = chunk_of(rows, 512)
    return pl.pallas_call(
        functools.partial(expand_kernel, keep),
        out_shape=jax.ShapeDtypeStruct((seq, rows), jnp.bfloat16),
        grid_spec=pltpu.PrefetchScalarGridSpec(
            num_scalar_prefetch=1,
            grid=(rows // step,),
            in_specs=[
                pl.BlockSpec((seq, width), lambda j, c: (0, 0)),
                pl.BlockSpec((step, keep * BLOCK), lambda j, c: (j, 0)),
            ],
            out_specs=pl.BlockSpec((seq, step), lambda j, c: (0, j)),
            scratch_shapes=[pltpu.VMEM((step, width), jnp.bfloat16)],
        ),
        compiler_params=pltpu.CompilerParams(vmem_limit_bytes=VMEM),
        cost_estimate=pl.CostEstimate(
            flops=2 * seq * rows * width,
            bytes_accessed=2 * rows * (seq + keep * BLOCK) + 2 * seq * width,
            transcendentals=0,
        ),
    )(cols.reshape(-1), x, blocks)


def kept_kernel(keep, pieces, base_ref, cols_ref, *refs):
    xs, ys = refs[:pieces], refs[pieces : 2 * pieces]
    out_ref, dense_ref = refs[2 * pieces :]
    j = pl.program_id(0)
    total = None
    for x_ref, y_ref in zip(xs, ys):
        term = lax.dot_general(
            x_ref[...], y_ref[...], (((0,), (0,)), ((), ())), preferred_element_type=jnp.float32
        )
        total = term if total is None else total + term
    dense_ref[...] = total
    block_rows = dense_ref.shape[0] // BLOCK
    for i in range(block_rows):
        rows = slice(i * BLOCK, (i + 1) * BLOCK)
        for k in range(keep):
            c = cols_ref[(j * block_rows + i) * keep + k]
            out_ref[rows, k * BLOCK : (k + 1) * BLOCK] = dense_ref[
                rows, pl.ds(pl.multiple_of(c * BLOCK, BLOCK), BLOCK)
            ]


def kept_product(wide, narrow, ys, position, cols):
    seq, rows = narrow[0].shape
    width = ys[0].shape[1]
    keep = cols.shape[1]
    step = chunk_of(rows, 256)
    steps = rows // step
    pieces = len(ys)
    xs = tuple(wide) + tuple(narrow)
    return pl.pallas_call(
        functools.partial(kept_kernel, keep, pieces),
        out_shape=jax.ShapeDtypeStruct((rows, keep * BLOCK), jnp.float32),
        grid_spec=pltpu.PrefetchScalarGridSpec(
            num_scalar_prefetch=2,
            grid=(steps,),
            in_specs=[pl.BlockSpec((seq, step), lambda j, b, c: (0, b[0] * steps + j))] * len(wide)
            + [pl.BlockSpec((seq, step), lambda j, b, c: (0, j))] * len(narrow)
            + [pl.BlockSpec((seq, width), lambda j, b, c: (0, 0))] * pieces,
            out_specs=pl.BlockSpec((step, keep * BLOCK), lambda j, b, c: (j, 0)),
            scratch_shapes=[pltpu.VMEM((step, width), jnp.float32)],
        ),
        compiler_params=pltpu.CompilerParams(vmem_limit_bytes=VMEM),
        cost_estimate=pl.CostEstimate(
            flops=2 * seq * pieces * rows * width,
            bytes_accessed=2 * seq * pieces * (rows + width) + 4 * rows * keep * BLOCK,
            transcendentals=0,
        ),
    )(position.reshape(1), cols.reshape(-1), *xs, *ys)


def state_mixer(projected, step_raw, conv_taps, step_bias, decay_rate, skip_gain, norm_gain):
    seq_steps = projected.shape[0]
    chan_count = projected.shape[1]
    inner_width = norm_gain.shape[0]
    head_count = step_bias.shape[0]
    head_width = inner_width // head_count
    state_size = (chan_count - inner_width) // 2
    taps = conv_taps.shape[0]
    padded = jnp.concatenate([jnp.zeros((taps - 1, chan_count), jnp.float32), projected], 0)
    conv_sum = jnp.zeros((seq_steps, chan_count), jnp.float32)
    for offset in range(taps):
        conv_sum = conv_sum + conv_taps[offset][None, :] * padded[offset : offset + seq_steps]
    activated = jax.nn.silu(conv_sum)
    head_inputs = activated[:, :inner_width].reshape(seq_steps, head_count, head_width)
    state_in = activated[:, inner_width : inner_width + state_size]
    state_out = activated[:, inner_width + state_size :]
    step_size = jax.nn.softplus(step_raw + step_bias[None, :])
    log_decay = jnp.cumsum(-decay_rate[None, :] * step_size, axis=0)
    scores = jnp.dot(state_out, state_in.T, precision=lax.Precision.HIGHEST)
    later = (jnp.arange(seq_steps)[:, None] >= jnp.arange(seq_steps)[None, :])[:, :, None]
    log_gap = log_decay[:, None, :] - log_decay[None, :, :]
    decay = jnp.where(later, jnp.exp(jnp.where(later, log_gap, 0.0)), 0.0)
    weights = scores[:, :, None] * decay * step_size[None, :, :]
    mixed = jnp.einsum("tsh,shp->thp", weights, head_inputs, precision=lax.Precision.HIGHEST)
    mixed = mixed + skip_gain[None, :, None] * head_inputs
    flat = mixed.reshape(seq_steps, inner_width)
    scale = lax.rsqrt(jnp.mean(flat * flat, axis=1, keepdims=True) + 1e-05)
    return flat * scale * norm_gain[None, :]


def shifted(value, axis, shift):
    size = lax.axis_size(axis)
    return lax.ppermute(value, axis, [(i, (i + shift) % size) for i in range(size)])


def after(value, *earlier):
    return lax.optimization_barrier((value,) + earlier)[0]


def local(
    tokens,
    teacher,
    in_blocks,
    in_columns,
    step_weight,
    out_blocks,
    out_columns,
    conv_weight,
    step_bias,
    decay_rate,
    skip_gain,
    norm_gain,
):
    my_tokens = tokens[0]
    my_teacher = teacher[0]
    seq_len, model_width = my_tokens.shape
    ring = lax.axis_size("fsdp")
    cores = lax.axis_size("dp")
    me = lax.axis_index("fsdp")
    core = lax.axis_index("dp")
    width = model_width // ring
    part = width // cores
    block_rows = part // BLOCK
    shifts = range(1, ring)

    def columns_for(value, shift):
        return lax.dynamic_slice_in_dim(value, lax.rem(me + shift, ring) * width, width, 1)

    def to_cores(values):
        sent = []
        for shift in range(1, cores):
            start = lax.rem(core + shift, cores) * part
            for value in values:
                piece = lax.dynamic_slice_in_dim(value, start, part, 1)
                sent.append(shifted(piece, "dp", shift))
        return sent

    def all_cores(values):
        return [shifted(value, "dp", shift) for shift in range(1, cores) for value in values]

    token_parts = [columns_for(my_tokens, 0)]
    token_parts += [shifted(columns_for(my_tokens, s), "fsdp", s) for s in shifts]

    in_own = contract(token_parts[0], in_blocks, in_columns, jnp.float32)
    raw_own = jnp.dot(token_parts[0], step_weight, preferred_element_type=jnp.float32)
    projected_sum, step_raw = in_own, raw_own
    for s in shifts:
        partial = contract(token_parts[s], in_blocks, in_columns, jnp.bfloat16)
        raw = jnp.dot(token_parts[s], step_weight, preferred_element_type=jnp.float32)
        projected_sum = projected_sum + shifted(partial, "fsdp", -s).astype(jnp.float32)
        step_raw = step_raw + shifted(raw, "fsdp", -s)
    projected = projected_sum.astype(jnp.bfloat16)

    def local_mix(values):
        return state_mixer(
            values, step_raw, conv_weight, step_bias, decay_rate, skip_gain, norm_gain
        )

    normed_exact, pull_back = jax.vjp(local_mix, projected.astype(jnp.float32))
    normed = normed_exact.astype(jnp.bfloat16)
    normed_parts = [normed] + [shifted(normed, "fsdp", s) for s in shifts]

    teacher_parts = [columns_for(my_teacher, 0)]
    teacher_parts += [
        shifted(after(columns_for(my_teacher, s), normed_parts[s]), "fsdp", s) for s in shifts
    ]
    token_rest = to_cores([after(value, normed) for value in token_parts])
    normed_rest = all_cores(normed_parts)

    total_tokens = seq_len * ring * cores
    grads, errors, backs = [], [], []
    students = []
    for value in normed_parts:
        term = expand(value, out_blocks, out_columns)
        if students:
            term = after(term, students[-1])
        students.append(lax.psum(term, "tensor"))
    for s in range(ring):
        gap = students[s].astype(jnp.float32) - teacher_parts[s].astype(jnp.float32)
        errors.append(jnp.sum(gap * gap, axis=1)[None, :])
        grads.append((gap * (1.0 / math.sqrt(total_tokens))).astype(jnp.bfloat16))
        backs.append(
            contract(
                grads[s], out_blocks, out_columns, jnp.float32 if s == 0 else jnp.bfloat16
            )
        )
    sq_error, d_normed = errors[0], backs[0]
    for s in shifts:
        d_normed = d_normed + shifted(backs[s], "fsdp", -s).astype(jnp.float32)
        sq_error = sq_error + shifted(errors[s], "fsdp", -s)
    sq_error = sq_error * (1.0 / model_width)

    in_pick = lax.dynamic_slice_in_dim(in_columns, core * block_rows, block_rows, 0)
    out_pick = lax.dynamic_slice_in_dim(out_columns, core * block_rows, block_rows, 0)
    grad_rest = to_cores(grads)
    out_grad = kept_product(grads, grad_rest, normed_parts + normed_rest, core, out_pick)

    d_projected = pull_back(d_normed)[0].astype(jnp.bfloat16)
    d_parts = [d_projected] + [shifted(d_projected, "fsdp", s) for s in shifts]
    d_rest = all_cores(d_parts)
    in_grad = kept_product(token_parts, token_rest, d_parts + d_rest, core, in_pick)
    return (sq_error, in_grad, out_grad)


def solution(mesh):
    placed = (
        P(("groups", "fsdp", "dp"), None, None),
        P(("groups", "fsdp", "dp"), None, None),
        P("fsdp", "tensor"),
        P("fsdp", "tensor"),
        P("fsdp", "tensor"),
        P("fsdp", "tensor"),
        P("fsdp", "tensor"),
        P(None, "tensor"),
        P("tensor"),
        P("tensor"),
        P("tensor"),
        P("tensor"),
    )
    return jax.shard_map(
        local,
        mesh=mesh,
        in_specs=placed,
        out_specs=(
            P(("groups", "fsdp", "dp"), None),
            P(("groups", "fsdp", "dp"), "tensor"),
            P(("groups", "fsdp", "dp"), "tensor"),
        ),
        check_vma=False,
    )
```

time: 1220 us -> 471 us (0.39)
  waiting for transfers between devices: 643 us -> 236 us
  local copies, waits for them, and re-layouts: 279 us -> 37.4 us
  matrix products: 199 us -> 41 us
  Pallas kernels: 0 us -> 107 us
  other arithmetic: 55.5 us -> 21.3 us
  blocking collectives: 20.1 us -> 0 us
  starting transfers between devices: 0.21 us -> 12.9 us
    all_gather x2 -> x0, waiting for transfers between devices: 357 us -> none  [the longest x1 190 us: local(): lax.all_gather(packed[0], 'fsdp', axis=0, tiled=True)]
    dot_general x8 -> x2, matrix products: 162 us -> 4.28 us  [the longest x1 2.93 us: local(): jnp.dot(token_parts[s], step_weight, preferred_element_type=jnp.float32)]
    reduce_scatter x2 -> x0, waiting for transfers between devices: 133 us -> none  [the longest x1 133 us: local(): lax.psum_scatter(in_term.astype(jnp.bfloat16), ('fsdp', 'dp'), scatter_di...]
    pallas_call x0 -> x8, Pallas kernels: none -> 107 us  [the longest x4 53 us: contract(): pl.pallas_call(functools.partial(contract_kernel, keep), out_shape=jax.Sh...]
    ppermute x0 -> x16, waiting for transfers between devices: none -> 98.4 us  [shifted(): lax.ppermute(value, axis, [(i, (i + shift) % size) for i in range(size)])]
    unnamed x56 -> x82, local copies, waits for them, and re-layouts: 84.6 us -> 8.11 us
    reshape x5, local copies, waits for them, and re-layouts: 69.5 us -> 0.37 us  [the longest x2 0.18 us: kept_product(): cols.reshape(-1)]
    gather x6 -> x0, local copies, waits for them, and re-layouts: 45.9 us -> none  [keep_blocks(): selected = jnp.take_along_axis(tile_grid, chosen[:, None, :, None], axis=2)]
  transfers between devices with their start and end apart: 5 -> 18, of which waited for: 4 -> 7; matrix products, arithmetic and copies ran while one was open for 24% -> 4% of each run, Pallas kernels for 0% -> 11%
where the time goes in v1:
time: 471 us; the launch traced here: 470 us
  waiting for transfers between devices  236 us (50%)
  Pallas kernels  107 us (23%)
  matrix products  41 us (9%)
  local copies, waits for them, and re-layouts  37.4 us (8%)
  other arithmetic  21.3 us (5%)
  between operations  14.5 us (3%)
  starting transfers between devices  12.9 us (3%)
    psum x2, waiting for transfers between devices, local(): students.append(lax.psum(term, 'tensor'))  137 us
    ppermute x16, waiting for transfers between devices, shifted(): lax.ppermute(value, axis, [(i, (i + shift) % size) for i in range(size)])  98.4 us
    pallas_call x4, Pallas kernels, contract(): pl.pallas_call(functools.partial(contract_kernel, keep), out_shape=jax.Sh...  53 us
    dot_general x3, matrix products, state_mixer(): jnp.einsum('tsh,shp->thp', weights, head_inputs, precision=lax.Precision....  33.6 us
    pallas_call x2, Pallas kernels, kept_product(): pl.pallas_call(functools.partial(kept_kernel, keep, pieces), out_shape=ja...  31.3 us
    pallas_call x2, Pallas kernels, expand(): pl.pallas_call(functools.partial(expand_kernel, keep), out_shape=jax.Shap...  22.6 us
    ppermute x16, starting transfers between devices, shifted(): lax.ppermute(value, axis, [(i, (i + shift) % size) for i in range(size)])  12.8 us
  transfers between devices with their start and end apart: 18, of which 7 were waited for; matrix products, arithmetic and copies ran while one was open for 4% of the time, Pallas kernels for 11%

profile of v1, /device:TPU:0, one launch (start us, length us, event | category | flops | bytes accessed | tf_op | source)
XLA Modules:
  0.0 469.9 jit_solution(18208459107955227435)
XLA Ops:
  7.3 4.1 dynamic-slice_bitcast_fusion.1
  11.3 2.9 collective-permute-start
  15.2 13.1 %shard_map.139 = f32[256,2304]{1,0:T(8,128)S(1)} custom-call(s32[288]{0:T(512)S(1)} %reshape.95.cols_ref, bf16[256,4096]{1,0:T(8,128)(2,1)S(1)} %get-tuple-element.9.x_ref.refs_0_, bf16[4096,1152]{1,0:T(8,128)(2,1)} %blocks_ref.7), custom_call_target="tpu_custom_call" | custom-call | flops 4831838208 | bytes 13893632 | tf_op jit(solution)/shard_map/pallas_call | solution.py:56
  29.7 30.5 %collective-permute-done.x_ref.refs_1_ = bf16[256,4096]{1,0:T(8,128)(2,1)} collective-permute-done((bf16[256,4096]{1,0:T(8,128)(2,1)}, bf16[256,4096]{1,0:T(8,128)(2,1)}, u32[]{:S(2)}, u32[]{:S(2)}) %collective-permute-start) | collective-permute-done | bytes 2097184 | tf_op jit(solution)/shard_map/ppermute | solution.py:198
  60.2 13.0 %shard_map.140 = bf16[256,2304]{1,0:T(8,128)(2,1)S(1)} custom-call(s32[288]{0:T(512)S(1)} %reshape.95.cols_ref, bf16[256,4096]{1,0:T(8,128)(2,1)} %collective-permute-done.x_ref.refs_1_, bf16[4096,1152]{1,0:T(8,128)(2,1)} %blocks_ref.7), custom_call_target="tpu_custom_call" | custom-call | flops 4831838208 | bytes 13893632 | tf_op jit(solution)/shard_map/pallas_call | solution.py:56
  76.4 2.9 fusion.34
  80.5 20.7 %collective-permute-done.2 = f32[256,32]{0,1:T(8,128)S(1)} collective-permute-done((f32[256,32]{0,1:T(8,128)}, f32[256,32]{0,1:T(8,128)S(1)}, u32[]{:S(2)}, u32[]{:S(2)}) %collective-permute-start.2) | collective-permute-done | bytes 32800 | tf_op jit(solution)/shard_map/ppermute | solution.py:198
  103.0 2.2 fusion.21
  105.3 2.8 fusion.19
  110.5 3.1 copy.26
  113.6 13.0 %multiply_reduce_fusion.3 = (f32[256]{0:T(256)S(1)}, f32[256,32,64]{0,2,1:T(8,128)}) fusion(f32[256,32,64]{0,2,1:T(8,128)} %bitcast.52, f32[32]{0:T(128)S(1)} %copy-done.39, f32[256,32]{0,1:T(8,128)S(1)} %get-tuple-element.18, f32[256,32]{0,1:T(8,128)S(1)} %bitcast_bitcast_fusion, f32[256,256]{1,0:T(8,128)S(1)} %fusion.24, ...), kind=kOutput, calls=%fused_computation.45 | convolution fusion | flops 1623195392 | bytes 4588672 | tf_op jit(solution)/shard_map/jvp(tsh,shp->thp)/dot_general | solution.py:189
  126.6 2.9 copy.29
  131.3 11.4 %shard_map.141 = bf16[256,4096]{1,0:T(8,128)(2,1)S(1)} custom-call(s32[256]{0:T(256)S(1)} %reshape.94.cols_ref, bf16[256,2048]{1,0:T(8,128)(2,1)S(1)} %multiply_convert_fusion.2.x_ref.refs_4_, bf16[4096,1024]{1,0:T(8,128)(2,1)} %blocks_ref.11), custom_call_target="tpu_custom_call" | custom-call | flops 4294967296 | bytes 11534336 | tf_op jit(solution)/shard_map/pallas_call | solution.py:94
  145.6 3.2 dynamic-slice_bitcast_fusion
  148.8 19.0 %collective-permute-done.3.x_ref.refs_5_ = bf16[256,2048]{1,0:T(8,128)(2,1)S(1)} collective-permute-done((bf16[256,2048]{1,0:T(8,128)(2,1)S(1)}, bf16[256,2048]{1,0:T(8,128)(2,1)S(1)}, u32[]{:S(2)}, u32[]{:S(2)}) %collective-permute-start.3) | collective-permute-done | bytes 1048608 | tf_op jit(solution)/shard_map/ppermute | solution.py:198
  168.8 11.2 %shard_map.142 = bf16[256,4096]{1,0:T(8,128)(2,1)S(1)} custom-call(s32[256]{0:T(256)S(1)} %reshape.94.cols_ref, bf16[256,2048]{1,0:T(8,128)(2,1)S(1)} %collective-permute-done.3.x_ref.refs_5_, bf16[4096,1024]{1,0:T(8,128)(2,1)} %blocks_ref.11), custom_call_target="tpu_custom_call" | custom-call | flops 4294967296 | bytes 11534336 | tf_op jit(solution)/shard_map/pallas_call | solution.py:94
  182.4 49.5 %all-reduce.11.cloned.1.call-done = bf16[256,4096]{1,0:T(8,128)(2,1)} async-done(((bf16[256,4096]{1,0:T(8,128)(2,1)}), bf16[256,4096]{1,0:T(8,128)(2,1)}) %all-reduce.11.cloned.1.call-update) | async-done | bytes 2097168 | tf_op jit(solution)/shard_map/psum | solution.py:282
  231.9 87.9 %all-reduce.13.cloned.1.call-done = bf16[256,4096]{1,0:T(8,128)(2,1)} async-done(((bf16[256,4096]{1,0:T(8,128)(2,1)}), bf16[256,4096]{1,0:T(8,128)(2,1)}) %all-reduce.13.cloned.1.call-update) | async-done | bytes 2097168 | tf_op jit(solution)/shard_map/psum | solution.py:282
  319.9 3.8 multiply_convert_fusion
  323.7 13.5 %shard_map.144 = bf16[256,2048]{1,0:T(8,128)(2,1)S(1)} custom-call(s32[256]{0:T(256)S(1)} %reshape.94.cols_ref, bf16[256,4096]{1,0:T(8,128)(2,1)S(1)} %get-tuple-element.23.x_ref.refs_1_, bf16[4096,1024]{1,0:T(8,128)(2,1)} %blocks_ref.11), custom_call_target="tpu_custom_call" | custom-call | flops 4294967296 | bytes 12582912 | tf_op jit(solution)/shard_map/pallas_call | solution.py:56
  339.8 13.3 %shard_map.143 = f32[256,2048]{1,0:T(8,128)S(1)} custom-call(s32[256]{0:T(256)S(1)} %reshape.94.cols_ref, bf16[256,4096]{1,0:T(8,128)(2,1)S(1)} %get-tuple-element.21.x_ref.refs_0_, bf16[4096,1024]{1,0:T(8,128)(2,1)} %blocks_ref.11), custom_call_target="tpu_custom_call" | custom-call | flops 4294967296 | bytes 12582912 | tf_op jit(solution)/shard_map/pallas_call | solution.py:56
  353.1 9.1 %collective-permute-done.8 = bf16[256,2048]{1,0:T(8,128)(2,1)S(1)} collective-permute-done((bf16[256,2048]{1,0:T(8,128)(2,1)S(1)}, bf16[256,2048]{1,0:T(8,128)(2,1)S(1)}, u32[]{:S(2)}, u32[]{:S(2)}) %collective-permute-start.8) | collective-permute-done | bytes 1048608 | tf_op jit(solution)/shard_map/ppermute | solution.py:198
  364.5 2.9 copy.33
  367.4 11.8 %fusion.1 = f32[256,256]{1,0:T(8,128)S(1)} fusion(f32[256,32]{0,1:T(8,128)S(1)} %copy-done.35, f32[256,32]{0,1:T(8,128)S(1)} %copy-done.33, pred[256,256]{1,0:T(8,128)(4,1)S(1)} %copy-done.28, f32[32,64,256]{2,1,0:T(8,128)} %bitcast.54, f32[256,32,64]{0,2,1:T(8,128)} %bitcast.53), kind=kOutput, calls=%fused_computation.2 | convolution fusion | flops 1623130112 | bytes 4587520 | tf_op jit(solution)/shard_map/transpose(jvp(tsh,shp->thp))/dot_general | solution.py:189
  382.0 8.8 %bitcast_add_fusion = f32[256,32,64]{0,2,1:T(8,128)} fusion(f32[256,32,64]{0,2,1:T(8,128)S(1)} %bitcast.55, f32[32,64,256]{2,1,0:T(8,128)S(1)} %bitcast.56, f32[256,32]{0,1:T(8,128)S(1)} %copy-done.35, f32[256,32]{0,1:T(8,128)S(1)} %copy-done.33, f32[256,256]{1,0:T(8,128)S(1)} %copy-done.19, pred[256,256]{1,0:T(8,128)(4,1)S(1)} %copy-done.28, ...), kind=kOutput, calls=%fused_computation.39 | convolution fusion | flops 1622147072 | bytes 6684800 | tf_op jit(solution)/shard_map/transpose(jvp(tsh,shp->thp))/dot_general | solution.py:189
  390.8 2.9 copy.34
  393.8 3.2 broadcast_multiply_fusion
  400.4 2.5 constant_dynamic-slice_fusion.1
  406.2 19.2 %collective-permute-done.9.refs_5_ = bf16[256,2304]{1,0:T(8,128)(2,1)} collective-permute-done((bf16[256,2304]{1,0:T(8,128)(2,1)S(1)}, bf16[256,2304]{1,0:T(8,128)(2,1)}, u32[]{:S(2)}, u32[]{:S(2)}) %collective-permute-start.9) | collective-permute-done | bytes 1179680 | tf_op jit(solution)/shard_map/ppermute | solution.py:198
  425.4 2.3 constant_dynamic-slice_fusion.3
  431.7 15.0 %shard_map.146 = f32[2048,1024]{1,0:T(8,128)} custom-call(s32[1]{0:T(128)} %bitcast.11.base_ref, s32[128]{0:T(128)S(1)} %reshape.104.cols_ref, bf16[256,4096]{1,0:T(8,128)(2,1)} %copy-done.5, bf16[256,4096]{1,0:T(8,128)(2,1)} %copy-done.3, bf16[256,2048]{1,0:T(8,128)(2,1)} %collective-permute-done.12.refs_2_, ...), custom_call_target="tpu_custom_call" | custom-call | flops 8589934592 | bytes 16777216 | tf_op jit(solution)/shard_map/pallas_call | solution.py:145
  446.8 16.2 %shard_map.145 = f32[2048,1152]{1,0:T(8,128)} custom-call(s32[1]{0:T(128)} %bitcast.11.base_ref, s32[144]{0:T(256)S(1)} %reshape.101.cols_ref, bf16[256,4096]{1,0:T(8,128)(2,1)} %copy-done.2, bf16[256,4096]{1,0:T(8,128)(2,1)} %collective-permute-done.x_ref.refs_1_, bf16[256,2048]{1,0:T(8,128)(2,1)} %collective-permute-done.6.refs_2_, ...), custom_call_target="tpu_custom_call" | custom-call | flops 9663676416 | bytes 18350080 | tf_op jit(solution)/shard_map/pallas_call | solution.py:145
  (146 shorter events, 37.3 us)
Async XLA Ops:
  7.2 67.9 %copy-start = (bf16[4096,32]{0,1:T(8,128)(2,1)S(1)}, bf16[4096,32]{0,1:T(8,128)(2,1)}, u32[]{:S(2)}) copy-start(bf16[4096,32]{0,1:T(8,128)(2,1)} %param.16) | copy-start | bytes 786436
  7.2 224.7 %all-reduce.11.cloned.1.call-start = ((), (), s32[]{:S(2)}) async-start(), calls=%async_computation | async-start | bytes 4194304 | tf_op jit(solution)/shard_map/psum | solution.py:282
  11.3 393.2 %copy-start.2 = (bf16[256,4096]{1,0:T(8,128)(2,1)}, bf16[256,4096]{1,0:T(8,128)(2,1)S(1)}, u32[]{:S(2)}) copy-start(bf16[256,4096]{1,0:T(8,128)(2,1)S(1)} %get-tuple-element.9.x_ref.refs_0_) | copy-start | bytes 6291460
  11.3 48.9 %collective-permute-start = (bf16[256,4096]{1,0:T(8,128)(2,1)}, bf16[256,4096]{1,0:T(8,128)(2,1)}, u32[]{:S(2)}, u32[]{:S(2)}) collective-permute-start(bf16[256,4096]{1,0:T(8,128)(2,1)} %get-tuple-element.25), channel_id=1, source_target_pairs={{0,2},{2,0},{1,3},{3,1},{4,6},{6,4},{5,7},{7,5},{8,10},{10,8},{9,1... | collective-permute-start | bytes 6291464 | tf_op jit(solution)/shard_map/ppermute | solution.py:198
  73.3 29.7 %collective-permute-start.1 = (bf16[256,2304]{1,0:T(8,128)(2,1)S(1)}, bf16[256,2304]{1,0:T(8,128)(2,1)}, u32[]{:S(2)}, u32[]{:S(2)}) collective-permute-start(bf16[256,2304]{1,0:T(8,128)(2,1)S(1)} %shard_map.140), channel_id=1, source_target_pairs={{0,2},{2,0},{1,3},{3,1},{4,6},{6,4},{5,7},{7,5},{8,10},{10,8},{9,1... | collective-permute-start | bytes 3538952 | tf_op jit(solution)/shard_map/ppermute | solution.py:198
  79.4 21.8 %collective-permute-start.2 = (f32[256,32]{0,1:T(8,128)}, f32[256,32]{0,1:T(8,128)S(1)}, u32[]{:S(2)}, u32[]{:S(2)}) collective-permute-start(f32[256,32]{0,1:T(8,128)} %fusion.34), channel_id=1, source_target_pairs={{0,2},{2,0},{1,3},{3,1},{4,6},{6,4},{5,7},{7,5},{8,10},{10,8},{9,1... | collective-permute-start | bytes 98312 | tf_op jit(solution)/shard_map/ppermute | solution.py:198
  79.7 33.9 %copy-start.27 = (pred[256,256]{1,0:T(8,128)(4,1)}, pred[256,256]{1,0:T(8,128)(4,1)S(1)}, u32[]{:S(2)}) copy-start(pred[256,256]{1,0:T(8,128)(4,1)S(1)} %iota_compare_fusion) | copy-start | bytes 196612
  110.5 16.1 %copy-start.18 = (f32[256,256]{1,0:T(8,128)}, f32[256,256]{1,0:T(8,128)S(1)}, u32[]{:S(2)}) copy-start(f32[256,256]{1,0:T(8,128)S(1)} %fusion.24) | copy-start | bytes 786436
  131.3 12.8 %copy-start.9 = (bf16[256,2048]{1,0:T(8,128)(2,1)}, bf16[256,2048]{1,0:T(8,128)(2,1)S(1)}, u32[]{:S(2)}) copy-start(bf16[256,2048]{1,0:T(8,128)(2,1)S(1)} %multiply_convert_fusion.2.x_ref.refs_4_) | copy-start | bytes 3145732
  144.1 175.8 %all-reduce.13.cloned.1.call-start = ((), (), s32[]{:S(2)}) async-start(), calls=%async_computation.1 | async-start | bytes 4194304 | tf_op jit(solution)/shard_map/psum | solution.py:282
  144.1 23.6 %collective-permute-start.3 = (bf16[256,2048]{1,0:T(8,128)(2,1)S(1)}, bf16[256,2048]{1,0:T(8,128)(2,1)S(1)}, u32[]{:S(2)}, u32[]{:S(2)}) collective-permute-start(bf16[256,2048]{1,0:T(8,128)(2,1)S(1)} %multiply_convert_fusion.2.x_ref.refs_4_), channel_id=1, source_target_pairs={{0,2},{2,0},{1,3},{3,1},{4,6},{6,4},{5,7},{7,5},{8,10},{10,8},{9,1... | collective-permute-start | bytes 3145736 | tf_op jit(solution)/shard_map/ppermute | solution.py:198
  167.7 64.2 %collective-permute-start.4 = (bf16[256,4096]{1,0:T(8,128)(2,1)}, bf16[256,4096]{1,0:T(8,128)(2,1)}, u32[]{:S(2)}, u32[]{:S(2)}) collective-permute-start(bf16[256,4096]{1,0:T(8,128)(2,1)} %dynamic-slice_bitcast_fusion), channel_id=1, source_target_pairs={{0,2},{2,0},{1,3},{3,1},{4,6},{6,4},{5,7},{7,5},{8,10},{10,8},{9,1... | collective-permute-start | bytes 6291464 | tf_op jit(solution)/shard_map/ppermute | solution.py:198
  323.7 13.5 %copy-start.3 = (bf16[256,4096]{1,0:T(8,128)(2,1)}, bf16[256,4096]{1,0:T(8,128)(2,1)S(1)}, u32[]{:S(2)}) copy-start(bf16[256,4096]{1,0:T(8,128)(2,1)S(1)} %get-tuple-element.23.x_ref.refs_1_) | copy-start | bytes 6291460
  323.7 15.0 %copy-start.15 = (bf16[1,256,8192]{2,1,0:T(8,128)(2,1)S(1)}, bf16[1,256,8192]{2,1,0:T(8,128)(2,1)}, u32[]{:S(2)}) copy-start(bf16[1,256,8192]{2,1,0:T(8,128)(2,1)} %param.13) | copy-start | bytes 12582916
  323.7 15.0 %copy-start.16 = (bf16[256,4096]{1,0:T(8,128)(2,1)S(1)}, bf16[256,4096]{1,0:T(8,128)(2,1)}, u32[]{:S(2)}) copy-start(bf16[256,4096]{1,0:T(8,128)(2,1)} %all-reduce.11.cloned.1.call-done) | copy-start | bytes 6291460
  337.2 25.0 %collective-permute-start.8 = (bf16[256,2048]{1,0:T(8,128)(2,1)S(1)}, bf16[256,2048]{1,0:T(8,128)(2,1)S(1)}, u32[]{:S(2)}, u32[]{:S(2)}) collective-permute-start(bf16[256,2048]{1,0:T(8,128)(2,1)S(1)} %shard_map.144), channel_id=1, source_target_pairs={{0,2},{2,0},{1,3},{3,1},{4,6},{6,4},{5,7},{7,5},{8,10},{10,8},{9,1... | collective-permute-start | bytes 3145736 | tf_op jit(solution)/shard_map/ppermute | solution.py:198
  339.8 13.3 %copy-start.5 = (bf16[256,4096]{1,0:T(8,128)(2,1)}, bf16[256,4096]{1,0:T(8,128)(2,1)S(1)}, u32[]{:S(2)}) copy-start(bf16[256,4096]{1,0:T(8,128)(2,1)S(1)} %get-tuple-element.21.x_ref.refs_0_) | copy-start | bytes 6291460
  339.8 22.4 %copy-start.13 = (f32[256,2048]{1,0:T(8,128)S(1)}, f32[256,2048]{1,0:T(8,128)}, u32[]{:S(2)}) copy-start(f32[256,2048]{1,0:T(8,128)} %copy.29) | copy-start | bytes 6291460
  367.4 14.6 %copy-start.17 = (f32[256,2048]{0,1:T(8,128)S(1)}, f32[256,2048]{0,1:T(8,128)}, u32[]{:S(2)}) copy-start(f32[256,2048]{0,1:T(8,128)} %copy.33) | copy-start | bytes 6291460
  367.4 14.6 %copy-start.19 = (f32[256,256]{1,0:T(8,128)S(1)}, f32[256,256]{1,0:T(8,128)}, u32[]{:S(2)}) copy-start(f32[256,256]{1,0:T(8,128)} %copy-done.18) | copy-start | bytes 786436
  398.4 27.0 %collective-permute-start.9 = (bf16[256,2304]{1,0:T(8,128)(2,1)S(1)}, bf16[256,2304]{1,0:T(8,128)(2,1)}, u32[]{:S(2)}, u32[]{:S(2)}) collective-permute-start(bf16[256,2304]{1,0:T(8,128)(2,1)S(1)} %fusion.18.refs_4_), channel_id=1, source_target_pairs={{0,2},{2,0},{1,3},{3,1},{4,6},{6,4},{5,7},{7,5},{8,10},{10,8},{9,1... | collective-permute-start | bytes 3538952 | tf_op jit(solution)/shard_map/ppermute | solution.py:198
  399.9 5.7 %collective-permute-start.14 = (bf16[256,2048]{1,0:T(8,128)(2,1)}, bf16[256,2048]{1,0:T(8,128)(2,1)}, u32[]{:S(2)}, u32[]{:S(2)}) collective-permute-start(bf16[256,2048]{1,0:T(8,128)(2,1)} %copy-done.9), channel_id=1, source_target_pairs={{0,1},{1,0},{2,3},{3,2},{4,5},{5,4},{6,7},{7,6},{8,9},{9,8},{10,11... | collective-permute-start | bytes 3145736 | tf_op jit(solution)/shard_map/ppermute | solution.py:198
  399.9 6.3 %collective-permute-start.15 = (bf16[256,2048]{1,0:T(8,128)(2,1)}, bf16[256,2048]{1,0:T(8,128)(2,1)}, u32[]{:S(2)}, u32[]{:S(2)}) collective-permute-start(bf16[256,2048]{1,0:T(8,128)(2,1)} %copy-done.11), channel_id=1, source_target_pairs={{0,1},{1,0},{2,3},{3,2},{4,5},{5,4},{6,7},{7,6},{8,9},{9,8},{10,11... | collective-permute-start | bytes 3145736 | tf_op jit(solution)/shard_map/ppermute | solution.py:198
  402.9 24.9 %collective-permute-start.12 = (bf16[256,2048]{1,0:T(8,128)(2,1)}, bf16[256,2048]{1,0:T(8,128)(2,1)}, u32[]{:S(2)}, u32[]{:S(2)}) collective-permute-start(bf16[256,2048]{1,0:T(8,128)(2,1)} %constant_dynamic-slice_fusion.1), channel_id=1, source_target_pairs={{0,1},{1,0},{2,3},{3,2},{4,5},{5,4},{6,7},{7,6},{8,9},{9,8},{10,11... | collective-permute-start | bytes 3145736 | tf_op jit(solution)/shard_map/ppermute | solution.py:198
  404.0 24.4 %copy-start.37 = (s32[32,8]{0,1:T(8,128)S(1)}, s32[32,8]{0,1:T(8,128)}, u32[]{:S(2)}) copy-start(s32[32,8]{0,1:T(8,128)} %param.18) | copy-start | bytes 3076
  404.0 25.3 %collective-permute-start.13 = (bf16[256,2048]{1,0:T(8,128)(2,1)}, bf16[256,2048]{1,0:T(8,128)(2,1)}, u32[]{:S(2)}, u32[]{:S(2)}) collective-permute-start(bf16[256,2048]{1,0:T(8,128)(2,1)} %constant_dynamic-slice_fusion), channel_id=1, source_target_pairs={{0,1},{1,0},{2,3},{3,2},{4,5},{5,4},{6,7},{7,6},{8,9},{9,8},{10,11... | collective-permute-start | bytes 3145736 | tf_op jit(solution)/shard_map/ppermute | solution.py:198
  405.6 22.6 %collective-permute-start.5 = (f32[1,256]{1,0:T(1,128)S(1)}, f32[1,256]{1,0:T(1,128)S(1)}, u32[]{:S(2)}, u32[]{:S(2)}) collective-permute-start(f32[1,256]{1,0:T(1,128)S(1)} %bitcast.61), channel_id=1, source_target_pairs={{0,2},{2,0},{1,3},{3,1},{4,6},{6,4},{5,7},{7,5},{8,10},{10,8},{9,1... | collective-permute-start | bytes 3080 | tf_op jit(solution)/shard_map/ppermute | solution.py:198
  406.2 40.6 %collective-permute-start.10 = (bf16[256,2304]{1,0:T(8,128)(2,1)S(1)}, bf16[256,2304]{1,0:T(8,128)(2,1)}, u32[]{:S(2)}, u32[]{:S(2)}) collective-permute-start(bf16[256,2304]{1,0:T(8,128)(2,1)S(1)} %fusion.18.refs_4_), channel_id=1, source_target_pairs={{0,1},{1,0},{2,3},{3,2},{4,5},{5,4},{6,7},{7,6},{8,9},{9,8},{10,11... | collective-permute-start | bytes 3538952 | tf_op jit(solution)/shard_map/ppermute | solution.py:198
  425.4 21.4 %collective-permute-start.11 = (bf16[256,2304]{1,0:T(8,128)(2,1)}, bf16[256,2304]{1,0:T(8,128)(2,1)}, u32[]{:S(2)}, u32[]{:S(2)}) collective-permute-start(bf16[256,2304]{1,0:T(8,128)(2,1)} %collective-permute-done.9.refs_5_), channel_id=1, source_target_pairs={{0,1},{1,0},{2,3},{3,2},{4,5},{5,4},{6,7},{7,6},{8,9},{9,8},{10,11... | collective-permute-start | bytes 3538952 | tf_op jit(solution)/shard_map/ppermute | solution.py:198
  427.7 19.1 %collective-permute-start.6 = (bf16[256,2048]{1,0:T(8,128)(2,1)}, bf16[256,2048]{1,0:T(8,128)(2,1)}, u32[]{:S(2)}, u32[]{:S(2)}) collective-permute-start(bf16[256,2048]{1,0:T(8,128)(2,1)} %constant_dynamic-slice_fusion.4), channel_id=1, source_target_pairs={{0,1},{1,0},{2,3},{3,2},{4,5},{5,4},{6,7},{7,6},{8,9},{9,8},{10,11... | collective-permute-start | bytes 3145736 | tf_op jit(solution)/shard_map/ppermute | solution.py:198
  428.2 18.5 %collective-permute-start.7 = (bf16[256,2048]{1,0:T(8,128)(2,1)}, bf16[256,2048]{1,0:T(8,128)(2,1)}, u32[]{:S(2)}, u32[]{:S(2)}) collective-permute-start(bf16[256,2048]{1,0:T(8,128)(2,1)} %constant_dynamic-slice_fusion.3), channel_id=1, source_target_pairs={{0,1},{1,0},{2,3},{3,2},{4,5},{5,4},{6,7},{7,6},{8,9},{9,8},{10,11... | collective-permute-start | bytes 3145736 | tf_op jit(solution)/shard_map/ppermute | solution.py:198
  446.8 16.2 %copy-start.1 = (bf16[4096,32]{0,1:T(8,128)(2,1)S(1)}, bf16[4096,32]{0,1:T(8,128)(2,1)}, u32[]{:S(2)}) copy-start(bf16[4096,32]{0,1:T(8,128)(2,1)} %param.16) | copy-start | bytes 786436
  (26 other events, 95.1 us)
Sparse Core Ops, SparseCore 0:
  144.2 87.6 all-reduce.10
  234.4 85.4 all-reduce.12
